TPU v7x, 32 devices: a whole 2x2x4 slice. The times are simulated.
32 devices in a mesh: groups: 2 (over y), dom: 4 (over z), sub: 2 (over x), chip: 2 (over core).
Axes of the slice: x: 2, y: 2, z: 4, core: 2. Of those that a mesh axis runs over, the one named last changes fastest.
Arguments:
- node_input: bfloat16 [32768, 128], P(('groups', 'dom', 'sub', 'chip')), parts along dimension 0, may hold values from -6 to 6
- fine_neighbours: int32 [8, 32768], P(None, ('groups', 'dom', 'sub', 'chip')), parts along dimension 1, may hold values from -128 to 128, as said below
- fine_edge_weight: float32 [8, 32768], P(None, ('groups', 'dom', 'sub', 'chip')), parts along dimension 1, may hold values from 0.05 to 0.5
- coarse_parent: int32 [32768], P(('groups', 'dom', 'sub', 'chip')), parts along dimension 0, may hold values from 0 to 8191, as said below
- restrict_weight: float32 [32768], P(('groups', 'dom', 'sub', 'chip')), parts along dimension 0, may hold values from 0.3 to 1
- prolong_weight: float32 [32768], P(('groups', 'dom', 'sub', 'chip')), parts along dimension 0, may hold values from 0.3 to 1
- coarse_neighbours: int32 [8, 16384], P(None, ('groups', 'dom', 'sub', 'chip')), parts along dimension 1, may hold values from -128 to 128, as said below
- coarse_edge_weight: float32 [8, 16384], P(None, ('groups', 'dom', 'sub', 'chip')), parts along dimension 1, may hold values from 0.05 to 0.5
- fine_target: float32 [4, 32768], P(None, ('groups', 'dom', 'sub', 'chip')), parts along dimension 1, may hold values from -6 to 6
- coarse_target: float32 [4, 16384], P(None, ('groups', 'dom', 'sub', 'chip')), parts along dimension 1, may hold values from -6 to 6
- proc_weight: bfloat16 [2, 3, 128, 128], replicated, may hold values from -0.5 to 0.5
- head_weight: bfloat16 [2, 4, 128], replicated, may hold values from -0.5 to 0.5
Outputs:
- input_grad: float32 [32768, 128], P(('groups', 'dom', 'sub', 'chip')), parts along dimension 0
- proc_grad: float32 [4, 3, 128, 128], P('groups'), parts along dimension 0
- head_grad: float32 [4, 4, 128], P('groups'), parts along dimension 0
There are 2 independent parts, one for each index of `groups`. A program takes and returns all parts, laid end to end along the dimension named above; an argument that names none is the same for every part. Nothing has to cross between parts.
Inputs may be any that keep to these rules, and one draw needn't show every extreme that they name: `fine_neighbours`: node i + entry [k, i] is a fine node of the window. `coarse_neighbours`: node i + entry [k, i] is a coarse node of the window. `coarse_parent`: for fine node i with parent p: p // 512 % 4 == i // 1024 % 4. Among the fine nodes of one aligned block of 1024 rows, at most 512 have parents with the same p // 2048, and exactly 512 do for one value.
All inputs are finite; a program needn't handle non-finite values.
Results may differ from a plain program's by a relative error of at most 0.018.
Values may be sent and summed in bfloat16 or wider, within the bound.
A program may use at most 64 MiB of HBM per device.

v0:
```python
import functools

import jax
import jax.numpy as jnp
from jax import lax
from jax.experimental import pallas as pl
from jax.experimental.pallas import tpu as pltpu
from jax.sharding import PartitionSpec as P

REACH = 128
MESH = pl.DeviceIdType.MESH
BF = jnp.bfloat16
F32 = jnp.float32


def dot(a, b):
    return jnp.dot(a, b, preferred_element_type=F32)


def dot_nt(a, b):
    return lax.dot_general(a, b, (((1,), (1,)), ((), ())), preferred_element_type=F32)


def dot_tn(a, b):
    return lax.dot_general(a, b, (((0,), (0,)), ((), ())), preferred_element_type=F32)


def build_band(nb_ref, ew_ref, band):
    base = lax.broadcasted_iota(jnp.int32, (3 * REACH, REACH), 0) - lax.broadcasted_iota(
        jnp.int32, (3 * REACH, REACH), 1
    )

    def body(b, carry):
        lanes = pl.ds(pl.multiple_of(b * REACH, REACH), REACH)
        total = jnp.zeros((3 * REACH, REACH), F32)
        for k in range(nb_ref.shape[0]):
            hit = base == nb_ref[k : k + 1, lanes] + REACH
            total = total + jnp.where(hit, ew_ref[k : k + 1, lanes], 0.0)
        band[b] = total.astype(BF)
        return carry

    lax.fori_loop(0, band.shape[0], body, 0)


def forward(ext, band, agg, act, slope, weights):
    blocks = band.shape[0]
    for b in range(blocks):
        agg[:, b * REACH : (b + 1) * REACH] = dot(
            ext[:, b * REACH : (b + 3) * REACH], band[b]
        ).astype(BF)
    feature = ext[:, REACH : (blocks + 1) * REACH]
    pre = dot_tn(weights[0], feature) + dot_tn(weights[1], agg[...])
    sigma = jax.nn.sigmoid(pre)
    act[...] = (pre * sigma).astype(BF)
    slope[...] = sigma * (1.0 + pre * (1.0 - sigma))
    return (feature.astype(F32) + dot_tn(weights[2], act[...])).astype(BF)


def kernel(
    dims,
    x_ref,
    fnb_ref,
    few_ref,
    parent_ref,
    restrict_ref,
    prolong_ref,
    cnb_ref,
    cew_ref,
    ft_ref,
    ct_ref,
    w_ref,
    head_ref,
    gin_ref,
    proc_ref,
    hgrad_ref,
    band_f,
    band_c,
    slots,
    pool_r,
    pool_p,
    ext_f,
    ext_c,
    halo_f,
    halo_c_out,
    halo_c,
    rim_f_out,
    rim_f,
    rim_c_out,
    rim_c,
    extra,
    extra_out,
    extra_in,
    slot_out,
    slot_in,
    back_out,
    back_in,
    joined_g,
    agg_f,
    act_f,
    slope_f,
    agg_c,
    act_c,
    slope_c,
    spread,
    gz_ref,
    up_f,
    up_c,
    acc,
    head8,
    gsum,
    ga_out,
    ga_in,
    gb_out,
    gb_in,
    gc_out,
    gc_in,
    gd_in,
    ring_send,
    ring_recv,
    dom_send,
    dom_recv,
    lane_send,
    lane_recv,
):
    D, S, H = dims
    L = S * H
    window = D * L
    rows = x_ref.shape[0]
    coarse = ct_ref.shape[1]
    nblk, blk = slots.shape[0], slots.shape[1]
    cpb = nblk // D
    cap = cpb * blk
    grp = lax.axis_index("groups")
    dom = lax.axis_index("dom")
    sub = lax.axis_index("sub")
    chip = lax.axis_index("chip")
    lane = sub * H + chip
    me = dom * L + lane

    def at_pos(p):
        return (grp, p // L, (p % L) // H, p % H)

    def at_dom(d):
        return (grp, d, sub, chip)

    def at_lane(q):
        return (grp, dom, q // H, q % H)

    left = at_pos((me + window - 1) % window)
    right = at_pos((me + 1) % window)

    barrier = pltpu.get_barrier_semaphore()
    peers = [left, right]
    peers += [at_dom((dom + o) % D) for o in range(1, D)]
    peers += [at_lane((lane + o) % L) for o in range(1, L)]
    for peer in peers:
        pl.semaphore_signal(barrier, inc=1, device_id=peer, device_id_type=MESH)
    pl.semaphore_wait(barrier, len(peers))

    started = []

    def send(src, dst, ssem, rsem, device):
        copy = pltpu.make_async_remote_copy(
            src_ref=src, dst_ref=dst, send_sem=ssem, recv_sem=rsem, device_id=device, device_id_type=MESH
        )
        copy.start()
        started.append(copy)

    def arrive(dst, ssem, rsem, device):
        pltpu.make_async_remote_copy(
            src_ref=dst, dst_ref=dst, send_sem=ssem, recv_sem=rsem, device_id=device, device_id_type=MESH
        ).wait_recv()

    def ring_start(stage, to_left, to_right, landing):
        send(to_right, landing.at[0], ring_send.at[stage, 0], ring_recv.at[stage, 0], right)
        send(to_left, landing.at[1], ring_send.at[stage, 1], ring_recv.at[stage, 1], left)

    def ring_wait(stage, landing):
        arrive(landing.at[0], ring_send.at[stage, 0], ring_recv.at[stage, 0], right)
        arrive(landing.at[1], ring_send.at[stage, 1], ring_recv.at[stage, 1], left)

    def dom_start(stage, off, src, dst):
        send(
            src, dst, dom_send.at[stage, off], dom_recv.at[stage, off], at_dom((dom + off) % D)
        )

    def dom_wait(stage, off, dst):
        arrive(dst, dom_send.at[stage, off], dom_recv.at[stage, off], at_dom((dom + off) % D))

    def part(d):
        return pl.ds(d * cpb, cpb)

    ring_start(0, x_ref.at[pl.ds(0, REACH)], x_ref.at[pl.ds(rows - REACH, REACH)], halo_f)

    parent = parent_ref[...]
    target = parent >> ((coarse * L).bit_length() - 1)
    local_row = parent & (coarse - 1)
    dpad = max(D, 16)
    onehot = (
        jnp.broadcast_to(target, (dpad, rows))
        == lax.broadcasted_iota(jnp.int32, (dpad, rows), 0)
    )
    onehot_f = jnp.where(onehot, 1.0, 0.0)
    upper = jnp.where(
        lax.broadcasted_iota(jnp.int32, (REACH, REACH), 0)
        <= lax.broadcasted_iota(jnp.int32, (REACH, REACH), 1),
        1.0,
        0.0,
    ).astype(BF)
    carry = jnp.zeros((dpad, 1), F32)
    within = []
    for b in range(rows // REACH):
        piece = onehot_f[:, b * REACH : (b + 1) * REACH]
        running = dot(piece.astype(BF), upper) + carry
        carry = carry + jnp.sum(piece, axis=1, keepdims=True)
        within.append(jnp.sum(piece * (running - 1.0), axis=0, keepdims=True))
    position = target * cap + jnp.concatenate(within, axis=1).astype(jnp.int32)

    extra[...] = jnp.zeros(extra.shape, F32)
    extra[0:4, :] = ft_ref[...]
    extra[4:5, :] = (local_row + 1).astype(F32)
    extra[5:6, :] = restrict_ref[...]
    extra[6:7, :] = prolong_ref[...]
    whole = extra[...]
    high = whole.astype(BF)
    rest = whole - high.astype(F32)
    middle = rest.astype(BF)
    low = (rest - middle.astype(F32)).astype(BF)
    slot_iota = lax.broadcasted_iota(jnp.int32, (blk, rows), 0)

    def slot_body(b, c):
        chosen = jnp.where(slot_iota == position - b * blk, 1.0, 0.0).astype(BF)
        slots[b] = chosen
        extra_out[b] = (dot_nt(high, chosen) + dot_nt(middle, chosen)) + dot_nt(low, chosen)
        return c

    lax.fori_loop(0, nblk, slot_body, 0)
    for off in range(1, D):
        dom_start(0, off, extra_out.at[part((dom + off) % D)], extra_in.at[part(dom)])
    extra_in[part(dom)] = extra_out[part(dom)]

    build_band(fnb_ref, few_ref, band_f)
    build_band(cnb_ref, cew_ref, band_c)
    head8[...] = jnp.zeros(head8.shape, F32)
    head8[0, 0:4, :] = head_ref[0].astype(F32)
    head8[1, 0:4, :] = head_ref[1].astype(F32)
    head_f = head8[0].astype(BF)
    head_c = head8[1].astype(BF)
    w_f = [w_ref[0, m] for m in range(3)]
    w_c = [w_ref[1, m] for m in range(3)]

    def turn(a):
        return jnp.transpose(a.astype(F32), (1, 0)).astype(BF)

    ext_f[:, REACH : REACH + rows] = turn(x_ref[...])
    ring_wait(0, halo_f)
    ext_f[:, 0:REACH] = turn(halo_f[0])
    ext_f[:, REACH + rows :] = turn(halo_f[1])
    out_f = forward(ext_f, band_f, agg_f, act_f, slope_f, w_f)

    for off in list(range(1, D)) + [0]:
        d = (dom + off) % D
        for c in range(cpb):
            b = d * cpb + c
            moved = dot_nt(out_f, slots[b]).astype(BF)
            if off:
                slot_out[b] = moved
            else:
                slot_in[b] = moved
        if off:
            dom_start(1, off, slot_out.at[part(d)], slot_in.at[part(dom)])

    for off in range(1, D):
        dom_wait(0, off, extra_in.at[part((dom + D - off) % D)])
    row_iota = lax.broadcasted_iota(jnp.int32, (coarse, blk), 0)

    def pool_body(b, c):
        info = extra_in[b]
        hit = row_iota == info[4:5, :].astype(jnp.int32) - 1
        pool_r[b] = jnp.where(hit, info[5:6, :], 0.0).astype(BF)
        pool_p[b] = jnp.where(hit, info[6:7, :], 0.0).astype(BF)
        return c

    lax.fori_loop(0, nblk, pool_body, 0)

    acc[...] = jnp.zeros(acc.shape, F32)
    for off in range(D):
        d = (dom + D - off) % D
        if off:
            dom_wait(1, off, slot_in.at[part(d)])
        for c in range(cpb):
            b = d * cpb + c
            acc[...] += dot_nt(slot_in[b], pool_r[b])
    ext_c[:, REACH : REACH + coarse] = acc[...].astype(BF)
    halo_c_out[0] = ext_c[:, REACH : 2 * REACH]
    halo_c_out[1] = ext_c[:, coarse : coarse + REACH]
    ring_start(1, halo_c_out.at[0], halo_c_out.at[1], halo_c)
    ring_wait(1, halo_c)
    ext_c[:, 0:REACH] = halo_c[0]
    ext_c[:, REACH + coarse :] = halo_c[1]
    out_c = forward(ext_c, band_c, agg_c, act_c, slope_c, w_c)

    top = lax.broadcasted_iota(jnp.int32, (8, blk), 0) < 4
    extra[:, 0:coarse] = jnp.zeros((8, coarse), F32)
    extra[0:4, 0:coarse] = ct_ref[...]
    errb_c = (dot(head_c, out_c) - extra[:, 0:coarse]).astype(BF)
    proc_rows = 6 * REACH
    gsum[proc_rows + 16 :] = jnp.zeros((gsum.shape[0] - proc_rows - 16, REACH), F32)
    gsum[proc_rows + 8 : proc_rows + 16] = dot_nt(errb_c, out_c)
    acc[...] = dot_tn(head_c, errb_c)

    def join_body(b, terms):
        joined = (slot_in[b].astype(F32) + dot(out_c, pool_p[b])).astype(BF)
        errb = (dot(head_f, joined) - jnp.where(top, extra_in[b], 0.0)).astype(BF)
        grad = dot_tn(head_f, errb).astype(BF)
        joined_g[b] = grad
        acc[...] += dot_nt(grad, pool_p[b])
        return terms + dot_nt(errb, joined)

    head_terms_f = lax.fori_loop(0, nblk, join_body, jnp.zeros((8, x_ref.shape[1]), F32))

    gsum[proc_rows : proc_rows + 8] = head_terms_f

    def backward(stage, up, band, agg, act, slope, feature, weights, rim_out, rim, level):
        blocks = band.shape[0]
        count = blocks * REACH
        gz = (dot(weights[2], up[...]) * slope[...]).astype(BF)
        gagg = dot(weights[1], gz).astype(BF)
        rim_out[0] = dot_nt(gagg[:, 0:REACH], band[0, 0:REACH]).astype(BF)
        rim_out[1] = dot_nt(gagg[:, count - REACH :], band[blocks - 1, 2 * REACH :]).astype(BF)
        ring_start(stage, rim_out.at[0], rim_out.at[1], rim)
        at = level * 3 * REACH
        gz_ref[:, 0:count] = gz
        gsum[at : at + 3 * REACH] = jnp.zeros((3 * REACH, REACH), F32)

        def grad_body(c, carry):
            lanes = pl.ds(pl.multiple_of(c * 512, 512), 512)
            part_z = gz_ref[:, lanes]
            shifted = pl.ds(pl.multiple_of(c * 512 + REACH, REACH), 512)
            gsum[at : at + REACH] += dot_nt(feature[:, shifted], part_z)
            gsum[at + REACH : at + 2 * REACH] += dot_nt(agg[:, lanes], part_z)
            gsum[at + 2 * REACH : at + 3 * REACH] += dot_nt(act[:, lanes], up[:, lanes])
            return carry

        lax.fori_loop(0, count // 512, grad_body, 0)
        grad = up[...].astype(F32) + dot(weights[0], gz)
        for b in range(blocks):
            lo, hi = max(b - 1, 0), min(b + 2, blocks)
            piece = dot_nt(
                gagg[:, b * REACH : (b + 1) * REACH],
                band[b, (lo - b + 1) * REACH : (hi - b + 1) * REACH],
            )
            if b == 0:
                spread[:, 0:count] = grad
            spread[:, lo * REACH : hi * REACH] += piece

    up_c[...] = acc[...].astype(BF)
    backward(
        2, up_c, band_c, agg_c, act_c, slope_c, ext_c, w_c, rim_c_out, rim_c, 1
    )
    ring_wait(2, rim_c)
    spread[:, 0:REACH] += rim_c[0].astype(F32)
    spread[:, coarse - REACH : coarse] += rim_c[1].astype(F32)
    grad_c = spread[:, 0:coarse].astype(BF)

    for off in list(range(1, D)) + [0]:
        d = (dom + off) % D
        for c in range(cpb):
            b = d * cpb + c
            moved = (joined_g[b].astype(F32) + dot(grad_c, pool_r[b])).astype(BF)
            if off:
                back_out[b] = moved
            else:
                back_in[b] = moved
        if off:
            dom_start(2, off, back_out.at[part(d)], back_in.at[part(dom)])

    spread[...] = jnp.zeros(spread.shape, F32)
    for off in range(D):
        d = (dom + D - off) % D
        if off:
            dom_wait(2, off, back_in.at[part(d)])
        for c in range(cpb):
            b = d * cpb + c
            spread[...] += dot(back_in[b], slots[b])
    up_f[...] = spread[...].astype(BF)
    backward(
        3, up_f, band_f, agg_f, act_f, slope_f, ext_f, w_f, rim_f_out, rim_f, 0
    )

    per_lane = ga_out.shape[1]
    per_dom = gb_out.shape[1]
    for q in range(L):
        ga_out[q] = gsum[q * per_lane : (q + 1) * per_lane].astype(BF)
    for off in range(1, L):
        send(
            ga_out.at[(lane + off) % L],
            ga_in.at[lane],
            lane_send.at[0, off],
            lane_recv.at[0, off],
            at_lane((lane + off) % L),
        )

    ring_wait(3, rim_f)
    spread[:, 0:REACH] += rim_f[0].astype(F32)
    spread[:, rows - REACH :] += rim_f[1].astype(F32)
    gin_ref[...] = jnp.transpose(spread[...], (1, 0))

    total = ga_out[lane].astype(F32)
    for off in range(1, L):
        q = (lane + L - off) % L
        arrive(ga_in.at[q], lane_send.at[0, off], lane_recv.at[0, off], at_lane((lane + off) % L))
        total = total + ga_in[q].astype(F32)
    for d in range(D):
        gb_out[d] = total[d * per_dom : (d + 1) * per_dom].astype(BF)
    for off in range(1, D):
        dom_start(3, off, gb_out.at[(dom + off) % D], gb_in.at[dom])
    mine = gb_out[dom].astype(F32)
    for off in range(1, D):
        d = (dom + D - off) % D
        dom_wait(3, off, gb_in.at[d])
        mine = mine + gb_in[d].astype(F32)
    gc_out[...] = mine.astype(BF)
    for off in range(1, D):
        dom_start(4, off, gc_out, gc_in.at[dom])
    gc_in[dom] = gc_out[...]
    for off in range(1, D):
        dom_wait(4, off, gc_in.at[(dom + D - off) % D])
    for off in range(1, L):
        send(
            gc_in,
            gd_in.at[lane],
            lane_send.at[1, off],
            lane_recv.at[1, off],
            at_lane((lane + off) % L),
        )
    gd_in[lane] = gc_in[...]
    for off in range(1, L):
        arrive(
            gd_in.at[(lane + L - off) % L],
            lane_send.at[1, off],
            lane_recv.at[1, off],
            at_lane((lane + off) % L),
        )
    scale = 1.0 / (rows * window)
    gsum[...] = gd_in[...].astype(F32).reshape(gsum.shape) * scale
    for m in range(6):
        proc_ref[m // 3, m % 3] = gsum[m * REACH : (m + 1) * REACH]
    hgrad_ref[0] = gsum[proc_rows : proc_rows + 4]
    hgrad_ref[1] = gsum[proc_rows + 8 : proc_rows + 12]
    for copy in started:
        copy.wait_send()


def per_device(dims, node_input, fnb, few, parent, restrict, prolong, cnb, cew, ft, ct, w, head):
    D, S, H = dims
    L = S * H
    rows, width = node_input.shape
    coarse = ct.shape[1]
    cap = 2 * rows // D
    blk = min(256, cap)
    nblk = 2 * rows // blk
    unit = 16 * L * D
    total = -(-(6 * REACH + 16) // unit) * unit
    fb, cb = rows // REACH, coarse // REACH
    vm = pltpu.VMEM
    scratch = [
        vm((fb, 3 * REACH, REACH), BF),
        vm((cb, 3 * REACH, REACH), BF),
        vm((nblk, blk, rows), BF),
        vm((nblk, coarse, blk), BF),
        vm((nblk, coarse, blk), BF),
        vm((width, rows + 2 * REACH), BF),
        vm((width, coarse + 2 * REACH), BF),
        vm((2, REACH, width), BF),
        vm((2, width, REACH), BF),
        vm((2, width, REACH), BF),
        vm((2, width, REACH), BF),
        vm((2, width, REACH), BF),
        vm((2, width, REACH), BF),
        vm((2, width, REACH), BF),
        vm((8, rows), F32),
        vm((nblk, 8, blk), F32),
        vm((nblk, 8, blk), F32),
        vm((nblk, width, blk), BF),
        vm((nblk, width, blk), BF),
        vm((nblk, width, blk), BF),
        vm((nblk, width, blk), BF),
        vm((nblk, width, blk), BF),
        vm((width, rows), BF),
        vm((width, rows), BF),
        vm((width, rows), F32),
        vm((width, coarse), BF),
        vm((width, coarse), BF),
        vm((width, coarse), F32),
        vm((width, rows), F32),
        vm((width, rows), BF),
        vm((width, rows), BF),
        vm((width, coarse), BF),
        vm((width, coarse), F32),
        vm((2, 8, width), F32),
        vm((total, width), F32),
        vm((L, total // L, width), BF),
        vm((L, total // L, width), BF),
        vm((D, total // L // D, width), BF),
        vm((D, total // L // D, width), BF),
        vm((total // L // D, width), BF),
        vm((D, total // L // D, width), BF),
        vm((L, D, total // L // D, width), BF),
        pltpu.SemaphoreType.DMA((4, 2)),
        pltpu.SemaphoreType.DMA((4, 2)),
        pltpu.SemaphoreType.DMA((5, D)),
        pltpu.SemaphoreType.DMA((5, D)),
        pltpu.SemaphoreType.DMA((2, L)),
        pltpu.SemaphoreType.DMA((2, L)),
    ]
    spec = pl.BlockSpec(memory_space=pltpu.VMEM)
    return pl.pallas_call(
        functools.partial(kernel, dims),
        out_shape=(
            jax.ShapeDtypeStruct((rows, width), F32),
            jax.ShapeDtypeStruct((2, 3, width, width), F32),
            jax.ShapeDtypeStruct((2, 4, width), F32),
        ),
        in_specs=[spec] * 12,
        out_specs=(spec, spec, spec),
        scratch_shapes=scratch,
        compiler_params=pltpu.CompilerParams(
            collective_id=0, has_side_effects=True, vmem_limit_bytes=50 * 1024 * 1024
        ),
    )(
        node_input,
        fnb,
        few,
        parent.reshape(1, rows),
        restrict.reshape(1, rows),
        prolong.reshape(1, rows),
        cnb,
        cew,
        ft,
        ct,
        w,
        head,
    )


def solution(mesh):
    dims = (mesh.shape["dom"], mesh.shape["sub"], mesh.shape["chip"])
    nodes = ("groups", "dom", "sub", "chip")
    return jax.shard_map(
        functools.partial(per_device, dims),
        mesh=mesh,
        in_specs=(
            P(nodes, None),
            P(None, nodes),
            P(None, nodes),
            P(nodes),
            P(nodes),
            P(nodes),
            P(None, nodes),
            P(None, nodes),
            P(None, nodes),
            P(None, nodes),
            P(),
            P(),
        ),
        out_specs=(
            P(nodes, None),
            P("groups", None, None, None),
            P("groups", None, None),
        ),
        check_vma=False,
    )
```

profile of v0, /device:TPU:0, one launch (start us, length us, event | category | flops | bytes accessed | tf_op | source)
XLA Modules:
  0.0 80.5 jit_solution(15353096467860994432)
XLA Ops:
  0.6 0.0 copy-start.8
  0.6 0.7 copy-done.8
  1.3 0.0 copy-start
  1.3 0.9 %copy-done = bf16[1024,128]{1,0:T(8,128)(2,1)S(1)} copy-done((bf16[1024,128]{1,0:T(8,128)(2,1)S(1)}, bf16[1024,128]{1,0:T(8,128)(2,1)}, u32[]{:S(2)}) %copy-start) | copy-done | bytes 262168
  2.3 0.0 copy-start.1
  2.3 0.9 %copy-done.1 = bf16[2,3,128,128]{3,2,1,0:T(8,128)(2,1)S(1)} copy-done((bf16[2,3,128,128]{3,2,1,0:T(8,128)(2,1)S(1)}, bf16[2,3,128,128]{3,2,1,0:T(8,128)(2,1)}, u32[]{:S(2)}) %copy-start.1) | copy-done | bytes 196632
  3.2 0.0 copy-start.2
  3.2 0.8 copy-done.2
  4.0 0.0 copy-start.3
  4.0 0.8 copy-done.3
  4.7 0.0 copy-start.4
  4.7 0.7 copy-done.4
  5.4 0.0 copy-start.5
  5.4 0.7 copy-done.5
  6.2 0.0 copy-start.6
  6.2 0.7 copy-done.6
  6.9 0.0 copy-start.7
  6.9 0.7 copy-done.7
  7.6 0.0 copy-start.9
  7.6 0.7 copy-done.9
  8.3 0.0 copy-start.10
  8.3 0.7 copy-done.10
  8.9 0.0 copy-start.11
  8.9 0.7 copy-done.11
  9.6 68.7 %shard_map.139 = (f32[1024,128]{1,0:T(8,128)S(1)}, f32[2,3,128,128]{3,2,1,0:T(8,128)S(1)}, f32[2,4,128]{2,1,0:T(4,128)S(1)}) custom-call(bf16[1024,128]{1,0:T(8,128)(2,1)S(1)} %copy-done, s32[8,1024]{1,0:T(8,128)S(1)} %copy-done.2, f32[8,1024]{1,0:T(8,128)S(1)} %copy-done.3, s32[1,1024]{1,0:T(1,128)S(1)} %bitcast.3, f32[1,1024]{1,0:T(1,128)S(1)} %bitcast.4, ...), custom_call_target="tpu_custom_call" | custom-call | tf_op jit(solution)/shard_map/pallas_call | solution.py:518
  78.4 0.8 copy.18
  79.2 0.7 copy.19
  79.9 0.6 copy.20
Async XLA Ops:
  0.6 0.7 copy-start.8
  1.3 0.9 %copy-start = (bf16[1024,128]{1,0:T(8,128)(2,1)S(1)}, bf16[1024,128]{1,0:T(8,128)(2,1)}, u32[]{:S(2)}) copy-start(bf16[1024,128]{1,0:T(8,128)(2,1)} %x_ref.1) | copy-start | bytes 786436
  2.3 0.9 %copy-start.1 = (bf16[2,3,128,128]{3,2,1,0:T(8,128)(2,1)S(1)}, bf16[2,3,128,128]{3,2,1,0:T(8,128)(2,1)}, u32[]{:S(2)}) copy-start(bf16[2,3,128,128]{3,2,1,0:T(8,128)(2,1)} %w_ref.1) | copy-start | bytes 589828
  3.2 0.8 copy-start.2
  4.0 0.8 copy-start.3
  4.7 0.7 copy-start.4
  5.4 0.7 copy-start.5
  6.2 0.7 copy-start.6
  6.9 0.7 copy-start.7
  7.6 0.7 copy-start.9
  8.3 0.7 copy-start.10
  8.9 0.7 copy-start.11
where the time goes:
time: 81.1 us; the launch traced here: 80.5 us
  Pallas kernels  68.7 us (85%)
  local copies, waits for them, and re-layouts  11.1 us (14%)
    pallas_call x1, Pallas kernels, per_device(): pl.pallas_call(functools.partial(kernel, dims), out_shape=(jax.ShapeDtype...  68.7 us
    unnamed x27, local copies, waits for them, and re-layouts  11.1 us

commit v1 on v0

--- a/solution.py
+++ b/solution.py
@@ -56,8 +56,21 @@
     return (feature.astype(F32) + dot_tn(weights[2], act[...])).astype(BF)
 
 
+def entry(dims, *refs):
+    held, local = refs[:12], refs[15:27]
+    copies = [
+        pltpu.make_async_copy(source, place, refs[27].at[i])
+        for i, (source, place) in enumerate(zip(held, local))
+    ]
+    for i in (3, 4, 5, 8, 1, 2, 0, 6, 7, 10, 11, 9):
+        copies[i].start()
+    kernel(dims, copies, held[0], *local, *refs[12:15], *refs[28:])
+
+
 def kernel(
     dims,
+    copies,
+    x_hbm,
     x_ref,
     fnb_ref,
     few_ref,
@@ -107,14 +120,16 @@
     up_c,
     acc,
     head8,
-    gsum,
-    ga_out,
-    ga_in,
-    gb_out,
-    gb_in,
-    gc_out,
-    gc_in,
-    gd_in,
+    gsum_f,
+    a_out_f,
+    a_in_f,
+    b_in_f,
+    d_in_f,
+    gsum_c,
+    a_out_c,
+    a_in_c,
+    b_in_c,
+    d_in_c,
     ring_send,
     ring_recv,
     dom_send,
@@ -179,19 +194,67 @@
         arrive(landing.at[0], ring_send.at[stage, 0], ring_recv.at[stage, 0], right)
         arrive(landing.at[1], ring_send.at[stage, 1], ring_recv.at[stage, 1], left)
 
-    def dom_start(stage, off, src, dst):
-        send(
-            src, dst, dom_send.at[stage, off], dom_recv.at[stage, off], at_dom((dom + off) % D)
-        )
-
-    def dom_wait(stage, off, dst):
-        arrive(dst, dom_send.at[stage, off], dom_recv.at[stage, off], at_dom((dom + off) % D))
+    arrivals = [0] + sorted(range(1, D), key=lambda o: (o & 1, o) if o != 1 else (0, D))
+    order = sorted(range(1, D), key=lambda o: (-o.bit_length(), o))
+
+    def mate(o):
+        d = dom
+        for k in range(o.bit_length()):
+            if (o >> k) & 1:
+                d = d + (1 - 2 * ((dom // 2**k) % 2)) * 2**k
+        return d
+
+    def dom_start(stage, o, src, dst):
+        send(src, dst, dom_send.at[stage, o], dom_recv.at[stage, o], at_dom(mate(o)))
+
+    def dom_wait(stage, o, dst):
+        arrive(dst, dom_send.at[stage, o], dom_recv.at[stage, o], at_dom(mate(o)))
+
+    def lane_start(stage, o, src, dst):
+        send(src, dst, lane_send.at[stage, o], lane_recv.at[stage, o], at_lane((lane + o) % L))
+
+    def lane_wait(stage, o, dst):
+        arrive(dst, lane_send.at[stage, o], lane_recv.at[stage, o], at_lane((lane + o) % L))
+
+    def sum_lanes(stage, source, a_out, a_in):
+        share = a_out.shape[1]
+        for q in range(L):
+            a_out[q] = source[q * share : (q + 1) * share].astype(BF)
+        for o in range(1, L):
+            lane_start(stage, o, a_out.at[(lane + o) % L], a_in.at[lane])
+
+    def sum_domains(stage, dom_stage, a_out, a_in, b_in):
+        total = a_out[lane].astype(F32)
+        for o in range(1, L):
+            q = (lane + L - o) % L
+            lane_wait(stage, o, a_in.at[q])
+            total = total + a_in[q].astype(F32)
+        b_in[dom] = total.astype(BF)
+        for o in order:
+            dom_start(dom_stage, o, b_in.at[dom], b_in.at[dom])
+
+    def share_sums(stage, dom_stage, b_in, d_in):
+        for o in order:
+            dom_wait(dom_stage, o, b_in.at[mate(o)])
+        total = b_in[0].astype(F32)
+        for d in range(1, D):
+            total = total + b_in[d].astype(F32)
+        d_in[lane] = total.astype(BF)
+        for o in range(1, L):
+            lane_start(stage, o, d_in.at[lane], d_in.at[lane])
+
+    def take_sums(stage, d_in, target):
+        for o in range(1, L):
+            lane_wait(stage, o, d_in.at[(lane + L - o) % L])
+        target[...] = d_in[...].astype(F32).reshape(target.shape) * (1.0 / (rows * window))
 
     def part(d):
         return pl.ds(d * cpb, cpb)
 
-    ring_start(0, x_ref.at[pl.ds(0, REACH)], x_ref.at[pl.ds(rows - REACH, REACH)], halo_f)
-
+    ring_start(0, x_hbm.at[pl.ds(0, REACH)], x_hbm.at[pl.ds(rows - REACH, REACH)], halo_f)
+
+    for i in (3, 4, 5, 8):
+        copies[i].wait()
     parent = parent_ref[...]
     target = parent >> ((coarse * L).bit_length() - 1)
     local_row = parent & (coarse - 1)
@@ -225,20 +288,26 @@
     high = whole.astype(BF)
     rest = whole - high.astype(F32)
     middle = rest.astype(BF)
-    low = (rest - middle.astype(F32)).astype(BF)
+    low = rest - middle.astype(F32)
+    thirds = jnp.concatenate(
+        [high.astype(F32), middle.astype(F32), low, jnp.zeros_like(low)], axis=0
+    ).astype(BF)
     slot_iota = lax.broadcasted_iota(jnp.int32, (blk, rows), 0)
 
     def slot_body(b, c):
         chosen = jnp.where(slot_iota == position - b * blk, 1.0, 0.0).astype(BF)
         slots[b] = chosen
-        extra_out[b] = (dot_nt(high, chosen) + dot_nt(middle, chosen)) + dot_nt(low, chosen)
+        found = dot_nt(thirds, chosen)
+        extra_out[b] = found[0:8] + found[8:16] + found[16:24]
         return c
 
     lax.fori_loop(0, nblk, slot_body, 0)
-    for off in range(1, D):
-        dom_start(0, off, extra_out.at[part((dom + off) % D)], extra_in.at[part(dom)])
+    for o in order:
+        dom_start(0, o, extra_out.at[part(mate(o))], extra_in.at[part(dom)])
     extra_in[part(dom)] = extra_out[part(dom)]
 
+    for i in (1, 2, 0, 6, 7, 10, 11, 9):
+        copies[i].wait()
     build_band(fnb_ref, few_ref, band_f)
     build_band(cnb_ref, cew_ref, band_c)
     head8[...] = jnp.zeros(head8.shape, F32)
@@ -258,8 +327,8 @@
     ext_f[:, REACH + rows :] = turn(halo_f[1])
     out_f = forward(ext_f, band_f, agg_f, act_f, slope_f, w_f)
 
-    for off in list(range(1, D)) + [0]:
-        d = (dom + off) % D
+    for off in order + [0]:
+        d = mate(off)
         for c in range(cpb):
             b = d * cpb + c
             moved = dot_nt(out_f, slots[b]).astype(BF)
@@ -270,8 +339,8 @@
         if off:
             dom_start(1, off, slot_out.at[part(d)], slot_in.at[part(dom)])
 
-    for off in range(1, D):
-        dom_wait(0, off, extra_in.at[part((dom + D - off) % D)])
+    for o in order:
+        dom_wait(0, o, extra_in.at[part(mate(o))])
     row_iota = lax.broadcasted_iota(jnp.int32, (coarse, blk), 0)
 
     def pool_body(b, c):
@@ -284,8 +353,8 @@
     lax.fori_loop(0, nblk, pool_body, 0)
 
     acc[...] = jnp.zeros(acc.shape, F32)
-    for off in range(D):
-        d = (dom + D - off) % D
+    for off in arrivals:
+        d = mate(off)
         if off:
             dom_wait(1, off, slot_in.at[part(d)])
         for c in range(cpb):
@@ -304,9 +373,10 @@
     extra[:, 0:coarse] = jnp.zeros((8, coarse), F32)
     extra[0:4, 0:coarse] = ct_ref[...]
     errb_c = (dot(head_c, out_c) - extra[:, 0:coarse]).astype(BF)
-    proc_rows = 6 * REACH
-    gsum[proc_rows + 16 :] = jnp.zeros((gsum.shape[0] - proc_rows - 16, REACH), F32)
-    gsum[proc_rows + 8 : proc_rows + 16] = dot_nt(errb_c, out_c)
+    head_at = 3 * REACH
+    if gsum_c.shape[0] > head_at + 16:
+        gsum_c[head_at + 16 :] = jnp.zeros((gsum_c.shape[0] - head_at - 16, REACH), F32)
+    gsum_c[head_at + 8 : head_at + 16] = dot_nt(errb_c, out_c)
     acc[...] = dot_tn(head_c, errb_c)
 
     def join_body(b, terms):
@@ -319,9 +389,9 @@
 
     head_terms_f = lax.fori_loop(0, nblk, join_body, jnp.zeros((8, x_ref.shape[1]), F32))
 
-    gsum[proc_rows : proc_rows + 8] = head_terms_f
-
-    def backward(stage, up, band, agg, act, slope, feature, weights, rim_out, rim, level):
+    gsum_c[head_at : head_at + 8] = head_terms_f
+
+    def backward(stage, up, band, agg, act, slope, feature, weights, rim_out, rim, gsum, then):
         blocks = band.shape[0]
         count = blocks * REACH
         gz = (dot(weights[2], up[...]) * slope[...]).astype(BF)
@@ -329,7 +399,7 @@
         rim_out[0] = dot_nt(gagg[:, 0:REACH], band[0, 0:REACH]).astype(BF)
         rim_out[1] = dot_nt(gagg[:, count - REACH :], band[blocks - 1, 2 * REACH :]).astype(BF)
         ring_start(stage, rim_out.at[0], rim_out.at[1], rim)
-        at = level * 3 * REACH
+        at = 0
         gz_ref[:, 0:count] = gz
         gsum[at : at + 3 * REACH] = jnp.zeros((3 * REACH, REACH), F32)
 
@@ -343,6 +413,7 @@
             return carry
 
         lax.fori_loop(0, count // 512, grad_body, 0)
+        then()
         grad = up[...].astype(F32) + dot(weights[0], gz)
         for b in range(blocks):
             lo, hi = max(b - 1, 0), min(b + 2, blocks)
@@ -356,15 +427,16 @@
 
     up_c[...] = acc[...].astype(BF)
     backward(
-        2, up_c, band_c, agg_c, act_c, slope_c, ext_c, w_c, rim_c_out, rim_c, 1
+        2, up_c, band_c, agg_c, act_c, slope_c, ext_c, w_c, rim_c_out, rim_c, gsum_c,
+        lambda: sum_lanes(2, gsum_c, a_out_c, a_in_c),
     )
     ring_wait(2, rim_c)
     spread[:, 0:REACH] += rim_c[0].astype(F32)
     spread[:, coarse - REACH : coarse] += rim_c[1].astype(F32)
     grad_c = spread[:, 0:coarse].astype(BF)
 
-    for off in list(range(1, D)) + [0]:
-        d = (dom + off) % D
+    for off in order + [0]:
+        d = mate(off)
         for c in range(cpb):
             b = d * cpb + c
             moved = (joined_g[b].astype(F32) + dot(grad_c, pool_r[b])).astype(BF)
@@ -376,78 +448,36 @@
             dom_start(2, off, back_out.at[part(d)], back_in.at[part(dom)])
 
     spread[...] = jnp.zeros(spread.shape, F32)
-    for off in range(D):
-        d = (dom + D - off) % D
+    for off in arrivals:
+        d = mate(off)
         if off:
             dom_wait(2, off, back_in.at[part(d)])
         for c in range(cpb):
             b = d * cpb + c
             spread[...] += dot(back_in[b], slots[b])
+    sum_domains(2, 4, a_out_c, a_in_c, b_in_c)
     up_f[...] = spread[...].astype(BF)
+    if gsum_f.shape[0] > 3 * REACH:
+        gsum_f[3 * REACH :] = jnp.zeros((gsum_f.shape[0] - 3 * REACH, REACH), F32)
     backward(
-        3, up_f, band_f, agg_f, act_f, slope_f, ext_f, w_f, rim_f_out, rim_f, 0
+        3, up_f, band_f, agg_f, act_f, slope_f, ext_f, w_f, rim_f_out, rim_f, gsum_f,
+        lambda: sum_lanes(0, gsum_f, a_out_f, a_in_f),
     )
 
-    per_lane = ga_out.shape[1]
-    per_dom = gb_out.shape[1]
-    for q in range(L):
-        ga_out[q] = gsum[q * per_lane : (q + 1) * per_lane].astype(BF)
-    for off in range(1, L):
-        send(
-            ga_out.at[(lane + off) % L],
-            ga_in.at[lane],
-            lane_send.at[0, off],
-            lane_recv.at[0, off],
-            at_lane((lane + off) % L),
-        )
-
+    sum_domains(0, 3, a_out_f, a_in_f, b_in_f)
+    share_sums(3, 4, b_in_c, d_in_c)
     ring_wait(3, rim_f)
     spread[:, 0:REACH] += rim_f[0].astype(F32)
     spread[:, rows - REACH :] += rim_f[1].astype(F32)
     gin_ref[...] = jnp.transpose(spread[...], (1, 0))
-
-    total = ga_out[lane].astype(F32)
-    for off in range(1, L):
-        q = (lane + L - off) % L
-        arrive(ga_in.at[q], lane_send.at[0, off], lane_recv.at[0, off], at_lane((lane + off) % L))
-        total = total + ga_in[q].astype(F32)
-    for d in range(D):
-        gb_out[d] = total[d * per_dom : (d + 1) * per_dom].astype(BF)
-    for off in range(1, D):
-        dom_start(3, off, gb_out.at[(dom + off) % D], gb_in.at[dom])
-    mine = gb_out[dom].astype(F32)
-    for off in range(1, D):
-        d = (dom + D - off) % D
-        dom_wait(3, off, gb_in.at[d])
-        mine = mine + gb_in[d].astype(F32)
-    gc_out[...] = mine.astype(BF)
-    for off in range(1, D):
-        dom_start(4, off, gc_out, gc_in.at[dom])
-    gc_in[dom] = gc_out[...]
-    for off in range(1, D):
-        dom_wait(4, off, gc_in.at[(dom + D - off) % D])
-    for off in range(1, L):
-        send(
-            gc_in,
-            gd_in.at[lane],
-            lane_send.at[1, off],
-            lane_recv.at[1, off],
-            at_lane((lane + off) % L),
-        )
-    gd_in[lane] = gc_in[...]
-    for off in range(1, L):
-        arrive(
-            gd_in.at[(lane + L - off) % L],
-            lane_send.at[1, off],
-            lane_recv.at[1, off],
-            at_lane((lane + off) % L),
-        )
-    scale = 1.0 / (rows * window)
-    gsum[...] = gd_in[...].astype(F32).reshape(gsum.shape) * scale
-    for m in range(6):
-        proc_ref[m // 3, m % 3] = gsum[m * REACH : (m + 1) * REACH]
-    hgrad_ref[0] = gsum[proc_rows : proc_rows + 4]
-    hgrad_ref[1] = gsum[proc_rows + 8 : proc_rows + 12]
+    share_sums(1, 3, b_in_f, d_in_f)
+    take_sums(3, d_in_c, gsum_c)
+    take_sums(1, d_in_f, gsum_f)
+    for m in range(3):
+        proc_ref[0, m] = gsum_f[m * REACH : (m + 1) * REACH]
+        proc_ref[1, m] = gsum_c[m * REACH : (m + 1) * REACH]
+    hgrad_ref[0] = gsum_c[head_at : head_at + 4]
+    hgrad_ref[1] = gsum_c[head_at + 8 : head_at + 12]
     for copy in started:
         copy.wait_send()
 
@@ -457,14 +487,26 @@
     L = S * H
     rows, width = node_input.shape
     coarse = ct.shape[1]
+    flat = [a.reshape(1, rows) for a in (parent, restrict, prolong)]
+    arguments = [node_input, fnb, few, *flat, cnb, cew, ft, ct, w, head]
     cap = 2 * rows // D
     blk = min(256, cap)
     nblk = 2 * rows // blk
-    unit = 16 * L * D
-    total = -(-(6 * REACH + 16) // unit) * unit
     fb, cb = rows // REACH, coarse // REACH
     vm = pltpu.VMEM
-    scratch = [
+    def sums(count):
+        share = -(-count // (16 * L)) * 16
+        return [
+            vm((L * share, width), F32),
+            vm((L, share, width), BF),
+            vm((L, share, width), BF),
+            vm((D, share, width), BF),
+            vm((L, share, width), BF),
+        ]
+
+    scratch = [vm(a.shape, a.dtype) for a in arguments]
+    scratch += [
+        pltpu.SemaphoreType.DMA((12,)),
         vm((fb, 3 * REACH, REACH), BF),
         vm((cb, 3 * REACH, REACH), BF),
         vm((nblk, blk, rows), BF),
@@ -499,49 +541,30 @@
         vm((width, coarse), BF),
         vm((width, coarse), F32),
         vm((2, 8, width), F32),
-        vm((total, width), F32),
-        vm((L, total // L, width), BF),
-        vm((L, total // L, width), BF),
-        vm((D, total // L // D, width), BF),
-        vm((D, total // L // D, width), BF),
-        vm((total // L // D, width), BF),
-        vm((D, total // L // D, width), BF),
-        vm((L, D, total // L // D, width), BF),
+        *sums(3 * REACH),
+        *sums(3 * REACH + 16),
         pltpu.SemaphoreType.DMA((4, 2)),
         pltpu.SemaphoreType.DMA((4, 2)),
         pltpu.SemaphoreType.DMA((5, D)),
         pltpu.SemaphoreType.DMA((5, D)),
-        pltpu.SemaphoreType.DMA((2, L)),
-        pltpu.SemaphoreType.DMA((2, L)),
+        pltpu.SemaphoreType.DMA((4, L)),
+        pltpu.SemaphoreType.DMA((4, L)),
     ]
     spec = pl.BlockSpec(memory_space=pltpu.VMEM)
     return pl.pallas_call(
-        functools.partial(kernel, dims),
+        functools.partial(entry, dims),
         out_shape=(
             jax.ShapeDtypeStruct((rows, width), F32),
             jax.ShapeDtypeStruct((2, 3, width, width), F32),
             jax.ShapeDtypeStruct((2, 4, width), F32),
         ),
-        in_specs=[spec] * 12,
+        in_specs=[pl.BlockSpec(memory_space=pl.ANY)] * 12,
         out_specs=(spec, spec, spec),
         scratch_shapes=scratch,
         compiler_params=pltpu.CompilerParams(
-            collective_id=0, has_side_effects=True, vmem_limit_bytes=50 * 1024 * 1024
+            collective_id=0, has_side_effects=True, vmem_limit_bytes=62 * 1024 * 1024
         ),
-    )(
-        node_input,
-        fnb,
-        few,
-        parent.reshape(1, rows),
-        restrict.reshape(1, rows),
-        prolong.reshape(1, rows),
-        cnb,
-        cew,
-        ft,
-        ct,
-        w,
-        head,
-    )
+    )(*arguments)
 
 
 def solution(mesh):

time: 81.1 us -> 64.3 us (0.79)
  Pallas kernels: 68.7 us -> 60.3 us
  local copies, waits for them, and re-layouts: 11.1 us -> 3.26 us
    pallas_call x1, Pallas kernels: 68.7 us -> 60.3 us  [per_device(): pl.pallas_call(functools.partial(entry, dims), out_shape=(jax.ShapeDtypeS...]
    unnamed x27 -> x7, local copies, waits for them, and re-layouts: 11.1 us -> 3.26 us
where the time goes in v1:
time: 64.3 us; the launch traced here: 64.2 us
  Pallas kernels  60.3 us (94%)
  local copies, waits for them, and re-layouts  3.26 us (5%)
  between operations  0.65 us (1%)
    pallas_call x1, Pallas kernels, per_device(): pl.pallas_call(functools.partial(entry, dims), out_shape=(jax.ShapeDtypeS...  60.3 us
    unnamed x7, local copies, waits for them, and re-layouts  3.26 us

profile of v1, /device:TPU:0, one launch (start us, length us, event | category | flops | bytes accessed | tf_op | source)
XLA Modules:
  0.0 64.2 jit_solution(3529836405039162069)
XLA Ops:
  0.6 60.3 %shard_map.139 = (f32[1024,128]{1,0:T(8,128)}, f32[2,3,128,128]{3,2,1,0:T(8,128)}, f32[2,4,128]{2,1,0:T(4,128)}) custom-call(bf16[1024,128]{1,0:T(8,128)(2,1)} %refs_0_.1, s32[8,1024]{1,0:T(8,128)} %refs_1_.1, f32[8,1024]{1,0:T(8,128)} %refs_2_.1, s32[1,1024]{1,0:T(1,128)} %bitcast.3, f32[1,1024]{1,0:T(1,128)} %bitcast.4, f32[1,1024]{1,0:T(1,128)} %bitcast.5, ...), custom_call_target="tpu_custom_call" | custom-call | tf_op jit(solution)/shard_map/pallas_call | solution.py:554
  60.9 0.0 copy-start
  60.9 1.9 %copy.18 = f32[1024,128]{1,0:T(8,128)} copy(f32[1024,128]{1,0:T(8,128)} %get-tuple-element.6) | data formatting | bytes 1048576
  62.8 0.0 copy-done
  62.8 0.0 copy-start.1
  62.8 0.7 %copy.19 = f32[2,3,128,128]{3,2,1,0:T(8,128)} copy(f32[2,3,128,128]{3,2,1,0:T(8,128)S(1)} %copy-done) | data formatting | bytes 786432
  63.6 0.0 copy-done.1
  63.6 0.6 copy.20
Async XLA Ops:
  60.9 1.9 %copy-start = (f32[2,3,128,128]{3,2,1,0:T(8,128)S(1)}, f32[2,3,128,128]{3,2,1,0:T(8,128)}, u32[]{:S(2)}) copy-start(f32[2,3,128,128]{3,2,1,0:T(8,128)} %get-tuple-element.7) | copy-start | bytes 1179652
  62.8 0.8 %copy-start.1 = (f32[2,4,128]{2,1,0:T(4,128)S(1)}, f32[2,4,128]{2,1,0:T(4,128)}, u32[]{:S(2)}) copy-start(f32[2,4,128]{2,1,0:T(4,128)} %get-tuple-element.8) | copy-start | bytes 12292
